TPU v7x, 128 devices: a whole 4x4x4 slice. The times are simulated.
128 devices in a mesh: worker: 8 (over x_lo, z), shard: 16 (over y, x_hi, core).
Axes of the slice: x: 4 (x_hi: 2, x_lo: 2; x = x_hi * 2 + x_lo), y: 4, z: 4, core: 2. Of those that a mesh axis runs over, the one named last changes fastest.
Arguments:
- token_ids: int32 [32768], P(('worker', 'shard')), may hold values from 0 to 16383, as said below
- cotangent: bfloat16 [32768, 1024], P(('worker', 'shard')), may hold values from -6 to 6
- embedding: bfloat16 [16384, 7168], P(('worker', 'shard')), may hold values from -6 to 6
- weight: bfloat16 [8, 7168, 1024], P('worker', 'shard'), may hold values from -6 to 6
- anchor: float32 [7168, 256], P('shard', 'worker'), may hold values from -6 to 6
- momentum: float32 [7168, 256], P('shard', 'worker'), may hold values from -3 to 3
- due_fragment: int32 [1], replicated, may hold values from 0 to 4095
Outputs:
- new_weight: bfloat16 [8, 7168, 1024], P('worker', 'shard')
- new_anchor: float32 [7168, 256], P('shard', 'worker')
- new_momentum: float32 [7168, 256], P('shard', 'worker')
Inputs may be any that keep to these rules, and one draw needn't show every extreme that they name: `token_ids`: among the 256 tokens of one device, at most 2 ids fall in any one device's block of 128 embedding rows, and exactly 2 fall in some block.
All inputs are finite; a program needn't handle non-finite values.
Results may differ from a plain program's by a relative error of at most 0.012.
Values may be sent and summed in bfloat16 or wider, within the bound.
A program may use at most 128 MiB of HBM per device.

v0:
```python
import jax
import jax.numpy as jnp
from jax import lax
from jax.sharding import PartitionSpec as P

epsilon = 1e-06
inner_rate = 1.0
outer_rate = 0.7
outer_decay = 0.9
mix_share = 0.5


def shards(token_ids, cotangent, embedding, weight, anchor, momentum, due_fragment):
    n_worker = lax.axis_size("worker")
    n_shard = lax.axis_size("shard")
    owners = n_worker * n_shard
    rows_per = embedding.shape[0]
    width = embedding.shape[1]
    tok_count = token_ids.shape[0]
    capacity = max(2, 5 * tok_count // (4 * owners))
    owner_dev = token_ids // rows_per
    matches = (owner_dev[:, None] == jnp.arange(owners, dtype=jnp.int32)[None, :]).astype(jnp.int32)
    position = jnp.sum(matches * (jnp.cumsum(matches, axis=0) - 1), axis=1)
    slot_index = owner_dev * capacity + position
    local_id = token_ids - owner_dev * rows_per
    requests = jnp.full((owners * capacity,), -1, jnp.int32).at[slot_index].set(local_id)
    asked = lax.all_to_all(
        requests.reshape(owners, capacity),
        ("worker", "shard"),
        split_axis=0,
        concat_axis=0,
        tiled=True,
    )
    valid = asked >= 0
    found = embedding[jnp.clip(asked, 0, rows_per - 1)]
    returned = lax.all_to_all(
        jnp.where(valid[..., None], found, jnp.zeros_like(found)),
        ("worker", "shard"),
        split_axis=0,
        concat_axis=0,
        tiled=True,
    )
    embedded = returned.reshape(owners * capacity, width)[slot_index].astype(jnp.float32)
    normed = (
        embedded * lax.rsqrt(jnp.mean(embedded * embedded, axis=1, keepdims=True) + epsilon)
    ).astype(jnp.bfloat16)
    weight_scale = width ** (-0.5)
    weight_local = weight[0]
    out_width = weight_local.shape[1]
    partial_value = jnp.dot(
        normed,
        lax.all_gather(weight_local, "shard", axis=0, tiled=True),
        preferred_element_type=jnp.float32,
    )
    preact = partial_value * weight_scale
    sig_val = jax.nn.sigmoid(preact)
    grad_pre = (cotangent.astype(jnp.float32) * sig_val * (1.0 + preact * (1.0 - sig_val))).astype(
        jnp.bfloat16
    )
    product = lax.dot_general(
        normed, grad_pre, (((0,), (0,)), ((), ())), preferred_element_type=jnp.float32
    )
    rounded = lax.optimization_barrier((product * weight_scale).astype(jnp.bfloat16))
    grads = lax.psum_scatter(
        rounded.astype(jnp.float32).astype(jnp.bfloat16), "shard", scatter_dimension=0, tiled=True
    ).astype(jnp.float32)
    stepped = weight_local.astype(jnp.float32) - inner_rate * grads
    frag_cols = anchor.shape[1] * n_worker
    frag_count = out_width // frag_cols
    col_start = due_fragment[0] % frag_count * frag_cols
    frag_own = lax.dynamic_slice_in_dim(weight_local, col_start, frag_cols, 1).astype(jnp.float32)
    summed = lax.psum_scatter(
        frag_own.astype(jnp.bfloat16), "worker", scatter_dimension=1, tiled=True
    ).astype(jnp.float32)
    replica_mean = summed / n_worker
    delta = anchor - replica_mean
    new_momentum = outer_decay * momentum + delta
    new_anchor = anchor - outer_rate * (delta + outer_decay * new_momentum)
    full_anchor = lax.all_gather(
        new_anchor.astype(jnp.bfloat16), "worker", axis=1, tiled=True
    ).astype(new_anchor.dtype)
    mixed = (
        mix_share * lax.dynamic_slice_in_dim(stepped, col_start, frag_cols, 1)
        + (1.0 - mix_share) * full_anchor
    )
    new_weight = lax.dynamic_update_slice_in_dim(stepped, mixed, col_start, 1).astype(jnp.bfloat16)
    return (new_weight[None], new_anchor, new_momentum)


def solution(mesh):
    placed = (
        P(("worker", "shard")),
        P(("worker", "shard"), None),
        P(("worker", "shard"), None),
        P("worker", "shard", None),
        P("shard", "worker"),
        P("shard", "worker"),
        P(),
    )
    return jax.shard_map(
        shards,
        mesh=mesh,
        in_specs=placed,
        out_specs=(P("worker", "shard", None), P("shard", "worker"), P("shard", "worker")),
        check_vma=False,
    )
```

profile of v0, /device:TPU:1, one launch (start us, length us, event | category | flops | bytes accessed | tf_op | source)
XLA Modules:
  0.0 322.7 jit_solution(10738661621604444894)
XLA Ops:
  8.0 0.0 copy-start
  8.0 0.0 all-gather.3.cloned.1.call-start
  8.1 0.7 all-gather.3.cloned.1.call-update
  8.7 0.7 multiply_subtract_fusion.2
  9.4 0.1 copy.44
  9.6 0.2 fusion.15
  9.8 0.1 add_add_fusion
  9.9 0.2 fusion.16
  10.1 1.4 scatter_custom_fusion
  11.5 0.1 all_to_all.9
  11.6 20.9 %all_to_all.14 = s32[128,1,2]{2,1,0:T(1,128)S(1)} all-to-all(s32[128,1,2]{2,1,0:T(1,128)S(1)} %bitcast.40), channel_id=1, replica_groups=mesh['worker'=8,'shard'=16] {'worker','shard'}, dimensions={0} | all-to-all | bytes 2048 | tf_op jit(solution)/shard_map/all_to_all | solution.py:27
  32.6 0.1 broadcast_clamp_fusion
  32.7 0.1 reshape.73
  32.8 0.0 copy-done
  32.9 4.7 %gather_fusion = bf16[256,7168]{1,0:T(8,128)(2,1)} fusion(bf16[128,7168]{1,0:T(8,128)(2,1)S(1)} %copy-done, s32[1024]{0:T(1024)S(1)} %pad_clamp_fusion.1), kind=kCustom, calls=%fused_computation | custom fusion | bytes 7341056 | tf_op jit(solution)/shard_map/gather | solution.py:35
  37.5 8.2 %reshape.72 = bf16[128,2,7168]{2,1,0:T(2,128)(2,1)} reshape(bf16[256,7168]{1,0:T(8,128)(2,1)} %gather_fusion) | data formatting | bytes 7340032 | tf_op jit(solution)/shard_map/gather | solution.py:35
  45.7 0.1 broadcast_compare_fusion
  45.7 0.1 copy.47
  45.8 0.1 copy.48
  46.0 7.0 %broadcast_select_fusion = bf16[128,2,7168]{2,1,0:T(2,128)(2,1)} fusion(bf16[128,2,7168]{2,1,0:T(2,128)(2,1)} %reshape.72, pred[128,2]{1,0:T(8,128)(4,1)S(1)} %copy.48), kind=kLoop, calls=%fused_computation.10 | loop fusion | flops 1835008 | bytes 7340288 | tf_op jit(solution)/shard_map/jit(_where)/select_n | solution.py:37
  53.0 0.0 copy-start.1
  53.0 5.2 %all-to-all-start.1 = ((bf16[128,2,7168]{2,1,0:T(2,128)(2,1)}), bf16[128,2,7168]{2,1,0:T(2,128)(2,1)}, u32[]{:S(2)}, u32[]{:S(2)}) async-start(bf16[128,2,7168]{2,1,0:T(2,128)(2,1)} %broadcast_select_fusion), calls=%async_computation.1 | async-start | bytes 7340032 | tf_op jit(solution)/shard_map/all_to_all | solution.py:36
  58.2 0.0 reduce-scatter.7.cloned.1.call-start
  58.9 0.0 copy-done.1
  59.0 0.8 copy.51
  59.8 0.0 reduce-scatter.7.cloned.1.call-update
  59.9 0.2 reduce-scatter.5.cloned.1.call-start
  60.1 81.3 %all-to-all-done.1 = bf16[128,2,7168]{2,1,0:T(2,128)(2,1)} async-done(((bf16[128,2,7168]{2,1,0:T(2,128)(2,1)}), bf16[128,2,7168]{2,1,0:T(2,128)(2,1)}, u32[]{:S(2)}, u32[]{:S(2)}) %all-to-all-start.1) | async-done | bytes 3670048 | tf_op jit(solution)/shard_map/all_to_all | solution.py:36
  141.4 8.4 %reshape.70 = bf16[256,7168]{1,0:T(8,128)(2,1)} reshape(bf16[128,2,7168]{2,1,0:T(2,128)(2,1)} %all-to-all-done.1) | data formatting | bytes 7340032 | tf_op jit(solution)/shard_map/reshape | solution.py:43
  149.8 10.5 %gather_fusion.1 = bf16[256,7168]{1,0:T(8,128)(2,1)} fusion(bf16[256,7168]{1,0:T(8,128)(2,1)} %reshape.70, s32[1024]{0:T(1024)S(1)} %pad_clamp_fusion), kind=kCustom, calls=%fused_computation.1 | custom fusion | bytes 7341056 | tf_op jit(solution)/shard_map/gather | solution.py:43
  160.3 0.0 copy-start.4
  160.3 2.9 fusion.2
  163.2 0.0 all-gather.3.cloned.1.call-done
  163.2 0.0 copy-done.4
  163.3 10.6 %multiply_convert_fusion.1 = bf16[256,1024]{1,0:T(8,128)(2,1)S(1)} fusion(bf16[256,1024]{1,0:T(8,128)(2,1)S(1)} %copy-done.4, bf16[1,7168,1024]{2,1,0:T(8,128)(2,1)} %all-gather.3.cloned.1.call-done, bf16[256,7168]{1,0:T(8,128)(2,1)} %gather_fusion.1, f32[256]{0:T(256)S(1)} %add_rsqrt_fusion), kind=kOutput, calls=%fused_computation.13 | convolution fusion | flops 3766484992 | bytes 19399680 | tf_op jit(solution)/shard_map/dot_general | solution.py:50
  173.9 10.0 %multiply_convert_fusion = bf16[7168,1024]{1,0:T(8,128)(2,1)} fusion(bf16[256,1024]{1,0:T(8,128)(2,1)S(1)} %multiply_convert_fusion.1, bf16[256,7168]{1,0:T(8,128)(2,1)} %gather_fusion.1, f32[256]{0:T(256)S(1)} %add_rsqrt_fusion), kind=kOutput, calls=%fused_computation.3 | convolution fusion | flops 3778281472 | bytes 18875392 | tf_op jit(solution)/shard_map/dot_general | solution.py:60
  183.9 0.0 copy-start.2
  183.9 0.0 copy-start.3
  183.9 0.0 reduce-scatter.5.cloned.1.call-update
  183.9 0.0 reduce-scatter.7.cloned.1.call-done
  183.9 0.8 copy-done.2
  184.7 0.0 copy-done.3
  184.7 1.4 fusion.21
  186.2 22.2 %all_gather.7 = bf16[448,256]{0,1:T(8,128)(2,1)S(1)} all-gather(bf16[448,32]{0,1:T(8,128)(2,1)S(1)} %get-tuple-element.15), channel_id=1, replica_groups=mesh['worker'=8,'shard'=16] {'worker'}, dimensions={1}, use_global_device_ids=true | all-gather | bytes 258048 | tf_op jit(solution)/shard_map/all_gather | solution.py:79
  208.3 0.1 copy.50
  208.5 104.1 %reduce-scatter.5.cloned.1.call-done = bf16[448,1024]{1,0:T(8,128)(2,1)} async-done(((bf16[7168,1024]{1,0:T(8,128)(2,1)}), bf16[448,1024]{1,0:T(8,128)(2,1)}) %reduce-scatter.5.cloned.1.call-update) | async-done | bytes 917520 | tf_op jit(solution)/shard_map/reduce_scatter | solution.py:64
  312.5 1.5 convert_subtract_fusion
  314.1 0.1 multiply_dynamic-update-slice_fusion
  314.2 1.1 convert_bitcast_fusion
  (10 shorter events, 0.1 us)
Async XLA Ops:
  8.0 24.8 %copy-start = (bf16[128,7168]{1,0:T(8,128)(2,1)S(1)}, bf16[128,7168]{1,0:T(8,128)(2,1)}, u32[]{:S(2)}) copy-start(bf16[128,7168]{1,0:T(8,128)(2,1)} %param.9) | copy-start | bytes 5505028
  8.0 155.2 %all-gather.3.cloned.1.call-start = ((), (), s32[]{:S(2)}) async-start(), calls=%async_computation.5 | async-start | bytes 15597568 | tf_op jit(solution)/shard_map/all_gather | solution.py:52
  53.0 5.9 %copy-start.1 = (bf16[1,448,1024]{2,1,0:T(8,128)(2,1)S(1)}, bf16[1,448,1024]{2,1,0:T(8,128)(2,1)}, u32[]{:S(2)}) copy-start(bf16[1,448,1024]{2,1,0:T(8,128)(2,1)} %param.10) | copy-start | bytes 2752516
  53.0 88.4 %all-to-all-start.1 = ((bf16[128,2,7168]{2,1,0:T(2,128)(2,1)}), bf16[128,2,7168]{2,1,0:T(2,128)(2,1)}, u32[]{:S(2)}, u32[]{:S(2)}) async-start(bf16[128,2,7168]{2,1,0:T(2,128)(2,1)} %broadcast_select_fusion), calls=%async_computation.1 | async-start | bytes 7340032 | tf_op jit(solution)/shard_map/all_to_all | solution.py:36
  58.2 125.7 %reduce-scatter.7.cloned.1.call-start = ((), (), s32[]{:S(2)}) async-start(), calls=%async_computation.6 | async-start | bytes 294912
  59.9 252.7 %reduce-scatter.5.cloned.1.call-start = ((), (), s32[]{:S(2)}) async-start(), calls=%async_computation.4 | async-start | bytes 15597568 | tf_op jit(solution)/shard_map/reduce_scatter | solution.py:64
  160.3 2.9 copy-start.4
  183.9 0.8 copy-start.2
  183.9 0.9 copy-start.3
Sparse Core Ops, SparseCore 0:
  11.6 140.3 all-gather.2
Sparse Core Ops, SparseCore 1:
  61.6 93.7 reduce-scatter.6
  184.0 128.5 reduce-scatter.4
where the time goes:
time: 324 us; the launch traced here: 323 us
  waiting for transfers between devices  186 us (57%)
  blocking collectives  43.1 us (13%)
  local copies, waits for them, and re-layouts  35.6 us (11%)
  matrix products  20.6 us (6%)
  between operations  16.3 us (5%)
  other arithmetic  15.4 us (5%)
  starting transfers between devices  5.52 us (2%)
    reduce_scatter x1, waiting for transfers between devices, shards(): lax.psum_scatter(rounded.astype(jnp.float32).astype(jnp.bfloat16), 'shard...  104 us
    all_to_all x1, waiting for transfers between devices, shards(): lax.all_to_all(jnp.where(valid[..., None], found, jnp.zeros_like(found)),...  81.3 us
    all_gather x1, blocking collectives, shards(): lax.all_gather(new_anchor.astype(jnp.bfloat16), 'worker', axis=1, tiled=T...  22.2 us
    all_to_all x1, blocking collectives, shards(): lax.all_to_all(requests.reshape(owners, capacity), ('worker', 'shard'), s...  20.9 us
    gather x2, local copies, waits for them, and re-layouts, shards(): found = embedding[jnp.clip(asked, 0, rows_per - 1)]  12.8 us
    dot_general x1, matrix products, shards(): jnp.dot(normed, lax.all_gather(weight_local, 'shard', axis=0, tiled=True)...  10.6 us
    gather x1, local copies, waits for them, and re-layouts, shards(): returned.reshape(owners * capacity, width)[slot_index].astype(jnp.float32)  10.5 us
    dot_general x1, matrix products, shards(): lax.dot_general(normed, grad_pre, (((0,), (0,)), ((), ())), preferred_ele...  9.96 us
  transfers between devices with their start and end apart: 4, of which 2 were waited for; matrix products, arithmetic and copies ran while one was open for 21% of the time, Pallas kernels for 0%

commit v1 on v0

v1 whole, which is shorter than its diff:
```python
import functools

import jax
import jax.numpy as jnp
from jax import lax
from jax.experimental import pallas as pl
from jax.experimental.pallas import tpu as pltpu
from jax.sharding import PartitionSpec as P

epsilon = 1e-06
inner_rate = 1.0
outer_rate = 0.7
outer_decay = 0.9
mix_share = 0.5

MESH = pl.DeviceIdType.MESH
f32, bf16, i32 = jnp.float32, jnp.bfloat16, jnp.int32


def iota(shape, dim):
    return lax.broadcasted_iota(i32, shape, dim)


def onehot(cond):
    return jnp.where(cond, 1.0, 0.0).astype(bf16)


def dot(a, b, ca=1, cb=0):
    return lax.dot_general(a, b, (((ca,), (cb,)), ((), ())), preferred_element_type=f32)


def m4(v):
    return lax.rem(v + 8, 4)


def kernel(
    ids_ref, fcol_ref, anchor_ref, mom_ref, emb_hbm, weight_hbm, cot_hbm,
    out_ref, new_anchor_ref, new_mom_ref,
    emb, normed, cot, ids_g, ids_all, SS, RA, RB, N, NT, WF,
    cot_send, cot_recv, cot_rows, fpad, f_send, f_recv, a_send, a_recv, full_anchor,
    acc, px_send, px_recv, G, PB, own_acc, CS, CR, S2, SL, SR, R2, RL, RR, nap,
    lsem, ssem, rsem,
):
    w = lax.axis_index("worker")
    s = lax.axis_index("shard")
    x_lo, z = w // 4, lax.rem(w, 4)
    y, x_hi, c = s // 4, lax.rem(s // 2, 2), lax.rem(s, 2)
    x = x_hi * 2 + x_lo
    width = emb.shape[1]
    half = width // 2
    chunk = width // 8
    scale = width ** (-0.5)
    rows = WF.shape[2]
    hr = rows // 2

    def dev(xx, yy, zz, cc):
        return (lax.rem(xx, 2) * 4 + zz, yy * 4 + (xx // 2) * 2 + cc)

    counter = [0]

    def send(src, dst, to):
        i = counter[0]
        counter[0] += 1
        copy = pltpu.make_async_remote_copy(
            src_ref=src, dst_ref=dst, send_sem=ssem.at[i], recv_sem=rsem.at[i],
            device_id=to, device_id_type=MESH,
        )
        copy.start()
        started.append(copy)
        return copy

    started = []

    zs = [dev(x, y, m4(z + d), c) for d in (1, 2, 3)]
    xs = [dev(m4(x + d), y, z, c) for d in (1, 2, 3)]
    x_flip = x_hi * 2 + 1 - x_lo
    workers = [(d, e) for d in (0, 1) for e in range(4) if (d, e) != (0, 0)]
    worker_of = lambda d, e: lax.rem(x_lo + d, 2) * 4 + m4(z + e)
    shards = [(d, h, k) for d in range(4) for h in (0, 1) for k in (0, 1) if (d, h, k) != (0, 0, 0)]
    shard_of = lambda d, h, k: m4(y + d) * 4 + lax.rem(x_hi + h, 2) * 2 + lax.rem(c + k, 2)

    emb_copy = pltpu.make_async_copy(emb_hbm, emb, lsem.at[0])
    weight_copy = pltpu.make_async_copy(weight_hbm, WF.at[y, c], lsem.at[1])
    cot_copy = pltpu.make_async_copy(cot_hbm, cot, lsem.at[2])
    emb_copy.start()
    weight_copy.start()
    cot_copy.start()

    barrier = pltpu.get_barrier_semaphore()
    n_partners = 0
    for d, e in workers:
        pl.semaphore_signal(barrier, inc=1, device_id=(worker_of(d, e), s), device_id_type=MESH)
        n_partners += 1
    for o in shards:
        pl.semaphore_signal(barrier, inc=1, device_id=(w, shard_of(*o)), device_id_type=MESH)
        n_partners += 1
    for d in (1, 3):
        pass
    pl.semaphore_signal(barrier, inc=1, device_id=dev(m4(x_flip + 2), y, z, c), device_id_type=MESH)
    n_partners += 1
    pl.semaphore_wait(barrier, n_partners)

    ids = ids_ref[...]
    ids_g[w] = jnp.broadcast_to(ids, (8, 256))
    first = [send(ids_g.at[w], ids_g.at[w], (worker_of(d, e), s)) for d, e in workers]

    emb_copy.wait()
    n_rows = emb.shape[0]
    total = jnp.zeros((n_rows, 128), f32)

    def add_square(t, total):
        v = emb[:, pl.ds(pl.multiple_of(t * 128, 128), 128)].astype(f32)
        return total + v * v

    total = lax.fori_loop(0, width // 128, add_square, total)
    factor = lax.rsqrt(jnp.sum(total, axis=1, keepdims=True) / width + epsilon)

    def scale_rows(t, carry):
        at = pl.ds(pl.multiple_of(t * 128, 128), 128)
        normed[:, at] = (emb[:, at].astype(f32) * factor).astype(bf16)
        return carry

    lax.fori_loop(0, width // 128, scale_rows, 0)

    for copy in first:
        copy.wait_recv()
    row8 = iota((8, 256), 0)
    tile = ids_g[0]
    for i in range(1, 8):
        tile = jnp.where(row8 == i, ids_g[i], tile)
    ids_all[s] = tile
    second = [send(ids_all.at[s], ids_all.at[s], (w, shard_of(*o))) for o in shards]

    sib = (w, s + 1 - 2 * c)
    up, down = (w, m4(y + 1) * 4 + lax.rem(s, 4)), (w, m4(y + 3) * 4 + lax.rem(s, 4))
    weight_copy.wait()
    for copy in second:
        copy.wait_recv()
    w_up = send(WF.at[y, c], WF.at[y, c], up)
    w_down = send(WF.at[y, c], WF.at[y, c], down)
    w_sib = [send(WF.at[y, c], WF.at[y, c], sib)]

    me = w * 16 + s
    asked = ids_all[...].reshape(128, 256)
    local = lax.rem(asked, 128).astype(f32)
    mine = (asked // 128) == me
    low = jnp.min(jnp.where(mine, local, 999.0), axis=1, keepdims=True)
    high = jnp.max(jnp.where(mine, local, -1.0), axis=1, keepdims=True)
    r_out, r_in = iota((128, 128), 0), iota((128, 128), 1)
    turn = onehot(r_in == lax.rem(r_out, 16) * 8 + r_out // 16)
    lane = iota((128, 128), 1).astype(f32)
    for k, pick in ((0, low), (1, high)):
        sel = dot(turn, onehot(lane == pick)).astype(bf16)
        for q in range(8):
            got = dot(sel, normed[:, q * chunk:(q + 1) * chunk]).astype(bf16)
            yq, h = q // 2, q % 2
            for ww in range(8):
                xd, zd = h * 2 + ww // 4, ww % 4
                a, b = (zd, xd) if k == 0 else (xd, zd)
                SS[k, a, b, :, yq * chunk:(yq + 1) * chunk] = got[ww * 16:(ww + 1) * 16]

    A, B, direct = [], [], []
    for d in (1, 3, 2):
        A.append((d, send(SS.at[0, m4(z + d)], RA.at[z], dev(x, y, m4(z + d), c))))
        B.append((d, send(SS.at[1, m4(x + d)], RB.at[x], dev(m4(x + d), y, z, c))))
    arrive = []
    for d in (1, 3, 2):
        arrive.append(send(SS.at[0, z, m4(x + d)], N.at[x, z, 0], dev(m4(x + d), y, z, c)))
        arrive.append(send(SS.at[1, x, m4(z + d)], N.at[x, z, 1], dev(x, y, m4(z + d), c)))
    N[x, z, 0] = SS[0, z, x]
    N[x, z, 1] = SS[1, x, z]

    cot_copy.wait()
    er, ec = iota((256, 256), 0), iota((256, 256), 1)
    idf = ids.astype(f32)
    id_row = jnp.broadcast_to(idf, (256, 256))
    id_col = jnp.sum(jnp.where(er == ec, id_row, 0.0), axis=1, keepdims=True)
    own_row = jnp.broadcast_to((ids // 128).astype(f32), (256, 256))
    own_col = jnp.sum(jnp.where(er == ec, own_row, 0.0), axis=1, keepdims=True)
    before = (own_col == own_row) & ((id_col < id_row) | ((id_col == id_row) & (er < ec)))
    rank = jnp.sum(jnp.where(before, 1.0, 0.0), axis=0, keepdims=True).astype(i32)
    owner = ids // 128
    place = lax.rem(owner, 16) * 16 + (owner // 16) * 2 + rank
    cot_send[...] = dot(onehot(er == place), cot[...]).astype(bf16).reshape(cot_send.shape)
    cots = [send(cot_send.at[shard_of(*o)], cot_recv.at[s], (w, shard_of(*o))) for o in shards]
    cot_recv[s] = cot_send[s]

    fcol = fcol_ref[...]
    due = [jnp.where(fcol == j, 1.0, 0.0) for j in range(4)]
    own_w = WF.at[y, c]
    frag = own_w[:, 0:256].astype(f32) * due[0]
    for j in range(1, 4):
        frag += own_w[:, j * 256:(j + 1) * 256].astype(f32) * due[j]
    fpad[rows:] = jnp.zeros((fpad.shape[0] - rows, 256), bf16)
    fpad[:rows] = frag.astype(bf16)
    eye = onehot(er == ec)
    f_send[...] = dot(eye, fpad[...], 1, 1).astype(bf16).reshape(f_send.shape)
    frags = [send(f_send.at[worker_of(d, e)], f_recv.at[w], (worker_of(d, e), s)) for d, e in workers]
    f_recv[w] = f_send[w]

    for (d, a), (_, b) in zip(A, B):
        a.wait_recv()
        zf = m4(z - d)
        for e in (1, 3, 2):
            arrive.append(send(RA.at[zf, m4(x + e)], N.at[x, zf, 0], dev(m4(x + e), y, z, c)))
        N[x, zf, 0] = RA[zf, x]
        b.wait_recv()
        xf = m4(x - d)
        for e in (1, 3, 2):
            arrive.append(send(RB.at[xf, m4(z + e)], N.at[xf, z, 1], dev(x, y, m4(z + e), c)))
        N[xf, z, 1] = RB[xf, z]

    yu, yd = m4(y + 1), m4(y + 3)
    y2 = m4(y + 2)
    w_up.wait_recv()
    w_far_up = send(WF.at[yd, c, 0:hr], WF.at[yd, c, 0:hr], up)
    w_sib.append(send(WF.at[yd, c], WF.at[yd, c], sib))
    w_down.wait_recv()
    w_far_down = send(WF.at[yu, c, hr:rows], WF.at[yu, c, hr:rows], down)
    w_sib.append(send(WF.at[yu, c], WF.at[yu, c], sib))
    w_far_up.wait_recv()
    w_sib.append(send(WF.at[y2, c, 0:hr], WF.at[y2, c, 0:hr], sib))
    w_far_down.wait_recv()
    w_sib.append(send(WF.at[y2, c, hr:rows], WF.at[y2, c, hr:rows], sib))

    for copy in frags:
        copy.wait_recv()
    sel32 = onehot(lax.rem(iota((256, 32), 0), 32) == iota((256, 32), 1))
    mean = dot(f_recv[...].reshape(256, 512), sel32, 0, 0)[:rows] / 8
    anchor = anchor_ref[...]
    delta = anchor - mean
    new_mom = outer_decay * mom_ref[...] + delta
    new_anchor = anchor - outer_rate * (delta + outer_decay * new_mom)
    new_mom_ref[...] = new_mom
    new_anchor_ref[...] = new_anchor
    nap[...] = jnp.zeros_like(nap)
    nap[:rows] = new_anchor.astype(bf16)
    eye32 = onehot(iota((32, 32), 0) == iota((32, 32), 1))
    a_send[...] = dot(eye32, nap[...], 1, 1).astype(bf16)
    anchors = [send(a_send, a_recv.at[w], (worker_of(d, e), s)) for d, e in workers]
    a_recv[w] = a_send[...]

    for copy in cots:
        copy.wait_recv()
    back = onehot(ec == lax.rem(er, 16) * 16 + er // 16)
    cot_rows[...] = dot(back, cot_recv[...].reshape(256, 1024)).astype(bf16)

    for copy in w_sib:
        copy.wait_recv()
    for copy in arrive:
        copy.wait_recv()

    cols = lambda j: slice(j * 256, (j + 1) * 256)
    x_pair = (w, y * 4 + (1 - x_hi) * 2 + c)
    px, gx, core, far, near = {}, {}, {}, {}, {}

    def forward(j):
        part = None
        for kk in range(4):
            a = N[:, :, :, :, kk * chunk:(kk + 1) * chunk].reshape(512, chunk)
            b = WF[kk].reshape(chunk, WF.shape[3])[:, cols(j)]
            p = dot(a, b)
            part = p if part is None else part + p
        acc[j % 2] = (part * scale).reshape(2, 256, 256)
        px_send[j] = acc[j % 2, 1 - x_hi].astype(bf16)
        px[j] = send(px_send.at[j], px_recv.at[j], x_pair)

    def pointwise(j):
        px[j].wait_recv()
        pre = acc[j % 2, x_hi] + px_recv[j].astype(f32)
        sig = jax.nn.sigmoid(pre)
        g = cot_rows[:, cols(j)].astype(f32) * sig * (1.0 + pre * (1.0 - sig))
        G[j, x_hi] = g.astype(bf16)
        gx[j] = send(G.at[j, x_hi], G.at[j, x_hi], x_pair)

    def turned():
        for q in range(half // 256):
            part = N[:, :, :, :, q * 256:(q + 1) * 256].reshape(512, 256)
            NT[q * 256:(q + 1) * 256] = dot(eye, part, 1, 1).astype(bf16)

    order = (2, 1, 3, 0)

    def backward(j):
        gx[j].wait_recv()
        g = G[j].reshape(512, 256)
        for d in order:
            yy = m4(y + d)
            base = yy * chunk
            other = NT[pl.ds(pl.multiple_of(base + (1 - c) * rows, 16), rows)]
            CS[j, d] = (dot(other, g) * scale).astype(bf16)
            core[j, d] = send(CS.at[j, d], CR.at[j, d], sib)
            own = NT[pl.ds(pl.multiple_of(base + c * rows, 16), rows)]
            PB[d] = dot(own, g) * scale

    def join(j):
        for d in order:
            core[j, d].wait_recv()
            t = PB[d] + CR[j, d].astype(f32)
            if d == 2:
                S2[j] = t.astype(bf16)
                far[j] = (
                    send(S2.at[j, 0:hr], R2.at[j, 0], up),
                    send(S2.at[j, hr:rows], R2.at[j, 1], down),
                )
            elif d == 1:
                SL[j, hr:rows] = t[hr:rows].astype(bf16)
                near[j] = [send(SL.at[j, hr:rows], RL.at[j, hr:rows], up)]
                PB[1, 0:hr] = t[0:hr]
            elif d == 3:
                SR[j, 0:hr] = t[0:hr].astype(bf16)
                near[j].append(send(SR.at[j, 0:hr], RR.at[j, 0:hr], down))
                PB[3, hr:rows] = t[hr:rows]
            else:
                own_acc[j] = t

    def pass_on(j):
        far[j][0].wait_recv()
        SL[j, 0:hr] = (PB[1, 0:hr] + R2[j, 0].astype(f32)).astype(bf16)
        near[j].append(send(SL.at[j, 0:hr], RL.at[j, 0:hr], up))
        far[j][1].wait_recv()
        SR[j, hr:rows] = (PB[3, hr:rows] + R2[j, 1].astype(f32)).astype(bf16)
        near[j].append(send(SR.at[j, hr:rows], RR.at[j, hr:rows], down))

    def finish(j):
        for copy in near[j]:
            copy.wait_recv()
        grads = own_acc[j] + RL[j].astype(f32) + RR[j].astype(f32)
        stepped = own_w[:, cols(j)].astype(f32) - inner_rate * grads
        share = due[j] * (1.0 - mix_share)
        out_ref[:, cols(j)] = (stepped * (1.0 - share) + share * full_anchor[...]).astype(bf16)

    forward(0)
    forward(1)
    turned()
    for copy in anchors:
        copy.wait_recv()
    full_anchor[...] = dot(a_recv[...].reshape(256, 512), eye, 0, 0)[:rows]
    pointwise(0)
    forward(2)
    pointwise(1)
    backward(0)
    join(0)
    pass_on(0)
    forward(3)
    pointwise(2)
    backward(1)
    join(1)
    pass_on(1)
    pointwise(3)
    backward(2)
    join(2)
    finish(0)
    pass_on(2)
    backward(3)
    join(3)
    finish(1)
    pass_on(3)
    finish(2)
    finish(3)

    for copy in started:
        copy.wait_send()


def shards(token_ids, cotangent, embedding, weight, anchor, momentum, due_fragment):
    rows, width = weight.shape[1], embedding.shape[1]
    half = width // 2
    fcol = jnp.full((1, 256), due_fragment[0] % 4, i32)
    vmem = pl.BlockSpec(memory_space=pltpu.VMEM)
    anyspace = pl.BlockSpec(memory_space=pl.ANY)
    V = pltpu.VMEM
    n_sends = 160
    new_weight, new_anchor, new_momentum = pl.pallas_call(
        kernel,
        out_shape=(
            jax.ShapeDtypeStruct((rows, 1024), bf16),
            jax.ShapeDtypeStruct(anchor.shape, f32),
            jax.ShapeDtypeStruct(anchor.shape, f32),
        ),
        in_specs=[vmem] * 4 + [anyspace] * 3,
        out_specs=(vmem, vmem, vmem),
        scratch_shapes=[
            V((128, width), bf16),
            V((128, width), bf16),
            V((256, 1024), bf16),
            V((8, 8, 256), i32),
            V((16, 8, 256), i32),
            V((2, 4, 4, 16, half), bf16),
            V((4, 4, 16, half), bf16),
            V((4, 4, 16, half), bf16),
            V((4, 4, 2, 16, half), bf16),
            V((half, 512), bf16),
            V((4, 2, rows, 1024), bf16),
            V((16, 16, 1024), bf16),
            V((16, 16, 1024), bf16),
            V((256, 1024), bf16),
            V((512, 256), bf16),
            V((8, 32, 512), bf16),
            V((8, 32, 512), bf16),
            V((32, 512), bf16),
            V((8, 32, 512), bf16),
            V((rows, 256), f32),
            V((2, 2, 256, 256), f32),
            V((4, 256, 256), bf16),
            V((4, 256, 256), bf16),
            V((4, 2, 256, 256), bf16),
            V((4, rows, 256), f32),
            V((4, rows, 256), f32),
            V((4, 4, rows, 256), bf16),
            V((4, 4, rows, 256), bf16),
            V((4, rows, 256), bf16),
            V((4, rows, 256), bf16),
            V((4, rows, 256), bf16),
            V((4, 2, rows // 2, 256), bf16),
            V((4, rows, 256), bf16),
            V((4, rows, 256), bf16),
            V((512, 32), bf16),
            pltpu.SemaphoreType.DMA((4,)),
            pltpu.SemaphoreType.DMA((n_sends,)),
            pltpu.SemaphoreType.DMA((n_sends,)),
        ],
        compiler_params=pltpu.CompilerParams(
            collective_id=0, has_side_effects=True, vmem_limit_bytes=60 * 2**20
        ),
        cost_estimate=pl.CostEstimate(flops=7_500_000_000, bytes_accessed=5_000_000, transcendentals=262144),
        name="diloco_step",
    )(token_ids.reshape(1, 256), fcol, anchor, momentum, embedding, weight.reshape(rows, 1024), cotangent)
    return (new_weight[None], new_anchor, new_momentum)


def solution(mesh):
    placed = (
        P(("worker", "shard")),
        P(("worker", "shard"), None),
        P(("worker", "shard"), None),
        P("worker", "shard", None),
        P("shard", "worker"),
        P("shard", "worker"),
        P(),
    )
    return jax.shard_map(
        shards,
        mesh=mesh,
        in_specs=placed,
        out_specs=(P("worker", "shard", None), P("shard", "worker"), P("shard", "worker")),
        check_vma=False,
    )
```

time: 324 us -> 139 us (0.43)
  waiting for transfers between devices: 186 us -> 0 us
  Pallas kernels: 0 us -> 128 us
  blocking collectives: 43.1 us -> 0 us
  local copies, waits for them, and re-layouts: 35.6 us -> 9.4 us
  matrix products: 20.6 us -> 0 us
  other arithmetic: 15.4 us -> 0 us
  between operations: 16.3 us -> 1.3 us
  starting transfers between devices: 5.52 us -> 0 us
    pallas_call x0 -> x1, Pallas kernels: none -> 128 us  [shards(): pl.pallas_call(kernel, out_shape=(jax.ShapeDtypeStruct((rows, 1024), bf16...]
    reduce_scatter x1 -> x0, waiting for transfers between devices: 104 us -> none  [shards(): lax.psum_scatter(rounded.astype(jnp.float32).astype(jnp.bfloat16), 'shard...]
    all_to_all x1 -> x0, waiting for transfers between devices: 81.3 us -> none  [shards(): lax.all_to_all(jnp.where(valid[..., None], found, jnp.zeros_like(found)),...]
    gather x3 -> x0, local copies, waits for them, and re-layouts: 23.3 us -> none  [the longest x2 12.8 us: shards(): found = embedding[jnp.clip(asked, 0, rows_per - 1)]]
    all_gather x1 -> x0, blocking collectives: 22.2 us -> none  [shards(): lax.all_gather(new_anchor.astype(jnp.bfloat16), 'worker', axis=1, tiled=T...]
    all_to_all x1 -> x0, blocking collectives: 20.9 us -> none  [shards(): lax.all_to_all(requests.reshape(owners, capacity), ('worker', 'shard'), s...]
    dot_general x2 -> x0, matrix products: 20.6 us -> none  [the longest x1 10.6 us: shards(): jnp.dot(normed, lax.all_gather(weight_local, 'shard', axis=0, tiled=True)...]
    reshape x1 -> x0, local copies, waits for them, and re-layouts: 8.44 us -> none  [shards(): returned.reshape(owners * capacity, width)[slot_index].astype(jnp.float32)]
  transfers between devices with their start and end apart: 4 -> 0, of which waited for: 2 -> 0; matrix products, arithmetic and copies ran while one was open for 21% -> 0% of each run, Pallas kernels for 0% -> 0%
where the time goes in v1:
time: 139 us; the launch traced here: 138 us
  Pallas kernels  128 us (92%)
  local copies, waits for them, and re-layouts  9.4 us (7%)
    pallas_call x1, Pallas kernels, shards(): pl.pallas_call(kernel, out_shape=(jax.ShapeDtypeStruct((rows, 1024), bf16...  128 us
    unnamed x5, local copies, waits for them, and re-layouts  8.84 us

profile of v1, /device:TPU:1, one launch (start us, length us, event | category | flops | bytes accessed | tf_op | source)
XLA Modules:
  0.0 138.5 jit_solution(6365965660190907395)
XLA Ops:
  1.3 0.6 broadcast_in_dim.6.fcol_ref
  1.9 1.7 %copy.10.anchor_ref = f32[448,32]{1,0:T(8,128)} copy(f32[448,32]{0,1:T(8,128)} %param.11) | data formatting | bytes 114688 | tf_op args[4]
  3.5 1.7 %copy.11.mom_ref = f32[448,32]{1,0:T(8,128)} copy(f32[448,32]{0,1:T(8,128)} %param.12) | data formatting | bytes 114688 | tf_op args[5]
  5.2 127.8 %diloco_step.1 = (bf16[448,1024]{1,0:T(8,128)(2,1)}, f32[448,32]{1,0:T(8,128)}, f32[448,32]{1,0:T(8,128)}) custom-call(s32[1,256]{1,0:T(1,128)} %bitcast.9, s32[1,256]{1,0:T(1,128)} %broadcast_in_dim.6.fcol_ref, f32[448,32]{1,0:T(8,128)} %copy.10.anchor_ref, f32[448,32]{1,0:T(8,128)} %copy.11.mom_ref, bf16[128,7168]{1,0:T(8,128)(2,1)} %emb_hbm.1, ...), custom_call_target="tpu_custom_call" | custom-call | flops 7500000256 | bytes 5000000 | tf_op jit(solution)/shard_map/diloco_step/pallas_call | solution.py:373
  133.0 1.7 %copy.12 = f32[448,32]{0,1:T(8,128)} copy(f32[448,32]{1,0:T(8,128)} %get-tuple-element.10) | data formatting | bytes 114688
  134.6 1.7 %copy.13 = f32[448,32]{0,1:T(8,128)} copy(f32[448,32]{1,0:T(8,128)} %get-tuple-element.11) | data formatting | bytes 114688
  136.3 2.2 %copy.16 = bf16[1,448,1024]{2,1,0:T(8,128)(2,1)} copy(bf16[1,448,1024]{2,1,0:T(8,128)(2,1)} %bitcast.7) | data formatting | bytes 1835008

commit v2 on v1

v2 whole, which is shorter than its diff:
```python
import functools

import jax
import jax.numpy as jnp
from jax import lax
from jax.experimental import pallas as pl
from jax.experimental.pallas import tpu as pltpu
from jax.sharding import PartitionSpec as P

epsilon = 1e-06
inner_rate = 1.0
outer_rate = 0.7
outer_decay = 0.9
mix_share = 0.5

MESH = pl.DeviceIdType.MESH
f32, bf16, i32 = jnp.float32, jnp.bfloat16, jnp.int32


def iota(shape, dim):
    return lax.broadcasted_iota(i32, shape, dim)


def onehot(cond):
    return jnp.where(cond, 1.0, 0.0).astype(bf16)


def dot(a, b, ca=1, cb=0):
    return lax.dot_general(a, b, (((ca,), (cb,)), ((), ())), preferred_element_type=f32)


def m4(v):
    return lax.rem(v + 8, 4)


def kernel(
    names, sizes,
    ids_ref, due_ref, anchor_ref, mom_ref, emb_hbm, weight_hbm, cot_hbm,
    out_hbm, new_anchor_ref, new_mom_ref, *scratch,
):
    R = dict(zip(names, scratch))
    emb, normed, cot, ids_g, ids_all = (R[n] for n in ("emb", "normed", "cot", "ids_g", "ids_all"))
    SS, RA, RB, N, NT, WF = (R[n] for n in ("SS", "RA", "RB", "N", "NT", "WF"))
    cot_send, cot_far, cot_recv, cot_rows = (R[n] for n in ("cot_send", "cot_far", "cot_recv", "cot_rows"))
    fpad, f_send, f_recv = (R[n] for n in ("fpad", "f_send", "f_recv"))
    a_send, a_recv, full_anchor = (R[n] for n in ("a_send", "a_recv", "full_anchor"))
    PB = R["PB"]
    lsem, ssem, rsem = R["lsem"], R["ssem"], R["rsem"]
    n_cols = len(sizes)
    starts = [sum(sizes[:j]) for j in range(n_cols)]
    w = lax.axis_index("worker")
    s = lax.axis_index("shard")
    x_lo, z = w // 4, lax.rem(w, 4)
    y, x_hi, c = s // 4, lax.rem(s // 2, 2), lax.rem(s, 2)
    x = x_hi * 2 + x_lo
    width = emb.shape[1]
    half = width // 2
    chunk = width // 8
    scale = width ** (-0.5)
    rows = WF.shape[2]
    hr = rows // 2

    def dev(xx, yy, zz, cc):
        return (lax.rem(xx, 2) * 4 + zz, yy * 4 + (xx // 2) * 2 + cc)

    counter = [0]

    def send(src, dst, to):
        i = counter[0]
        counter[0] += 1
        copy = pltpu.make_async_remote_copy(
            src_ref=src, dst_ref=dst, send_sem=ssem.at[i], recv_sem=rsem.at[i],
            device_id=to, device_id_type=MESH,
        )
        copy.start()
        started.append(copy)
        return copy

    started = []

    def done(until=None):
        for copy in started:
            copy.wait_send()

    zs = [dev(x, y, m4(z + d), c) for d in (1, 2, 3)]
    xs = [dev(m4(x + d), y, z, c) for d in (1, 2, 3)]
    x_flip = x_hi * 2 + 1 - x_lo
    hops = (0, 1, 2, 1)
    workers = [(d, e) for d in (0, 1) for e in range(4) if (d, e) != (0, 0)]
    workers.sort(key=lambda o: -(o[0] + hops[o[1]]))
    worker_of = lambda d, e: lax.rem(x_lo + d, 2) * 4 + m4(z + e)
    shards = [(d, h, k) for d in range(4) for h in (0, 1) for k in (0, 1) if (d, h, k) != (0, 0, 0)]
    shards.sort(key=lambda o: -(2 * hops[o[0]] + 4 * o[1] + o[2]))
    shard_of = lambda d, h, k: m4(y + d) * 4 + lax.rem(x_hi + h, 2) * 2 + lax.rem(c + k, 2)

    emb_copy = pltpu.make_async_copy(emb_hbm, emb, lsem.at[0])
    weight_copy = pltpu.make_async_copy(weight_hbm, WF.at[y, c], lsem.at[1])
    cot_copy = pltpu.make_async_copy(cot_hbm, cot, lsem.at[2])
    emb_copy.start()
    weight_copy.start()
    cot_copy.start()

    barrier = pltpu.get_barrier_semaphore()
    n_partners = 0
    for d, e in workers:
        pl.semaphore_signal(barrier, inc=1, device_id=(worker_of(d, e), s), device_id_type=MESH)
        n_partners += 1
    for o in shards:
        pl.semaphore_signal(barrier, inc=1, device_id=(w, shard_of(*o)), device_id_type=MESH)
        n_partners += 1
    pl.semaphore_signal(barrier, inc=1, device_id=dev(m4(x_flip + 2), y, z, c), device_id_type=MESH)
    n_partners += 1
    pl.semaphore_wait(barrier, n_partners)

    ids = ids_ref[...]
    ids_g[w] = jnp.broadcast_to(ids, (8, 256))
    first = [send(ids_g.at[w], ids_g.at[w], (worker_of(d, e), s)) for d, e in workers]

    cot_copy.wait()
    er, ec = iota((256, 256), 0), iota((256, 256), 1)
    idf = ids.astype(f32)
    id_row = jnp.broadcast_to(idf, (256, 256))
    id_col = jnp.sum(jnp.where(er == ec, id_row, 0.0), axis=1, keepdims=True)
    owner = ids >> 7
    own_row = jnp.broadcast_to(owner.astype(f32), (256, 256))
    own_col = jnp.sum(jnp.where(er == ec, own_row, 0.0), axis=1, keepdims=True)
    before = (own_col == own_row) & ((id_col < id_row) | ((id_col == id_row) & (er < ec)))
    rank = jnp.sum(jnp.where(before, 1.0, 0.0), axis=0, keepdims=True).astype(i32)
    turn_s = ((owner & 12) + ((owner & 1) << 1) + ((owner >> 1) & 1))
    place = turn_s * 16 + (owner >> 4) * 2 + rank
    cot_send[...] = dot(onehot(er == place), cot[...]).astype(bf16).reshape(cot_send.shape)
    x_pair = (w, y * 4 + (1 - x_hi) * 2 + c)
    s_pair = s + 2 - 4 * x_hi
    cot_x = [send(cot_send.at[0:3], cot_far.at[0:3], x_pair)]
    lines = [(d, k) for d in (2, 1, 3, 0) for k in (1, 0) if (d, k) != (0, 0)]
    pair_of = lambda d, k: m4(y + d) * 2 + lax.rem(c + k, 2)
    line_of = lambda d, k: (w, m4(y + d) * 4 + x_hi * 2 + lax.rem(c + k, 2))
    cots = [send(cot_send.at[pair_of(*o)], cot_recv.at[s], line_of(*o)) for o in lines]
    cot_recv[s] = cot_send[y * 2 + c]
    for copy in first:
        copy.wait_recv()
    row8 = iota((8, 256), 0)
    tile = ids_g[0]
    for i in range(1, 8):
        tile = jnp.where(row8 == i, ids_g[i], tile)
    ids_all[s] = tile
    second = [send(ids_all.at[s], ids_all.at[s], (w, shard_of(*o))) for o in shards]

    cot_x.append(send(cot_send.at[3:8], cot_far.at[3:8], x_pair))
    weight_copy.wait()
    fcol = jnp.full((1, 256), lax.rem(due_ref[0], 4), i32)
    due = [jnp.where(fcol == j, 1.0, 0.0) for j in range(4)]
    own_w = WF.at[y, c]
    frag = own_w[:, 0:256].astype(f32) * due[0]
    for j in range(1, 4):
        frag += own_w[:, j * 256:(j + 1) * 256].astype(f32) * due[j]
    fpad[rows:] = jnp.zeros((fpad.shape[0] - rows, 256), bf16)
    fpad[:rows] = frag.astype(bf16)
    eye = onehot(er == ec)
    f_send[...] = dot(eye, fpad[...], 1, 1).astype(bf16).reshape(f_send.shape)
    f_recv[w] = f_send[w]
    frags = [send(f_send.at[worker_of(d, e)], f_recv.at[w], (worker_of(d, e), s)) for d, e in workers]

    emb_copy.wait()
    n_rows = emb.shape[0]
    total = jnp.zeros((n_rows, 128), f32)

    def add_square(t, total):
        v = emb[:, pl.ds(pl.multiple_of(t * 128, 128), 128)].astype(f32)
        return total + v * v

    total = lax.fori_loop(0, width // 128, add_square, total, unroll=8)
    factor = lax.rsqrt(jnp.sum(total, axis=1, keepdims=True) / width + epsilon)

    def scale_rows(t, carry):
        at = pl.ds(pl.multiple_of(t * 128, 128), 128)
        normed[:, at] = (emb[:, at].astype(f32) * factor).astype(bf16)
        return carry

    lax.fori_loop(0, width // 128, scale_rows, 0, unroll=8)

    for copy in second:
        copy.wait_recv()

    me = w * 16 + s
    asked = ids_all[...].reshape(128, 256)
    local = (asked & 127).astype(f32)
    mine = (asked >> 7) == me
    low = jnp.min(jnp.where(mine, local, 999.0), axis=1, keepdims=True)
    high = jnp.max(jnp.where(mine, local, -1.0), axis=1, keepdims=True)
    r_out, r_in = iota((128, 128), 0), iota((128, 128), 1)
    turn = onehot(r_in == (r_out & 15) * 8 + (r_out >> 4))
    lane = iota((128, 128), 1).astype(f32)
    A, B = [], []
    for k, pick in ((0, low), (1, high)):
        sel = dot(turn, onehot(lane == pick)).astype(bf16)
        for q in range(8):
            got = dot(sel, normed[:, q * chunk:(q + 1) * chunk]).astype(bf16)
            yq, h = q // 2, q % 2
            for ww in range(8):
                xd, zd = h * 2 + ww // 4, ww % 4
                a, b = (zd, xd) if k == 0 else (xd, zd)
                SS[k, a, b, :, yq * chunk:(yq + 1) * chunk] = got[ww * 16:(ww + 1) * 16]
        for d in (1, 3, 2):
            if k == 0:
                A.append((d, send(SS.at[0, m4(z + d)], RA.at[z], dev(x, y, m4(z + d), c))))
            else:
                B.append((d, send(SS.at[1, m4(x + d)], RB.at[x], dev(m4(x + d), y, z, c))))

    arrive = []
    for d in (1, 3, 2):
        arrive.append(send(SS.at[0, z, m4(x + d)], N.at[x, z, 0], dev(m4(x + d), y, z, c)))
        arrive.append(send(SS.at[1, x, m4(z + d)], N.at[x, z, 1], dev(x, y, m4(z + d), c)))
    N[x, z, 0] = SS[0, z, x]
    N[x, z, 1] = SS[1, x, z]

    sib = (w, s + 1 - 2 * c)
    up, down = (w, m4(y + 1) * 4 + lax.rem(s, 4)), (w, m4(y + 3) * 4 + lax.rem(s, 4))
    w_up = send(WF.at[y, c], WF.at[y, c], up)
    w_down = send(WF.at[y, c], WF.at[y, c], down)
    w_sib = [send(WF.at[y, c], WF.at[y, c], sib)]

    for copy in cot_x:
        copy.wait_recv()
    cots += [send(cot_far.at[pair_of(*o)], cot_recv.at[s_pair], line_of(*o)) for o in lines]
    cot_recv[s_pair] = cot_far[y * 2 + c]
    for (d, a), (_, b) in zip(A, B):
        a.wait_recv()
        zf = m4(z - d)
        for e in (1, 3, 2):
            arrive.append(send(RA.at[zf, m4(x + e)], N.at[x, zf, 0], dev(m4(x + e), y, z, c)))
        N[x, zf, 0] = RA[zf, x]
        b.wait_recv()
        xf = m4(x - d)
        for e in (1, 3, 2):
            arrive.append(send(RB.at[xf, m4(z + e)], N.at[xf, z, 1], dev(x, y, m4(z + e), c)))
        N[xf, z, 1] = RB[xf, z]

    yu, yd = m4(y + 1), m4(y + 3)
    y2 = m4(y + 2)
    w_up.wait_recv()
    w_far_up = send(WF.at[yd, c, 0:hr], WF.at[yd, c, 0:hr], up)
    w_sib.append(send(WF.at[yd, c], WF.at[yd, c], sib))
    w_down.wait_recv()
    w_far_down = send(WF.at[yu, c, hr:rows], WF.at[yu, c, hr:rows], down)
    w_sib.append(send(WF.at[yu, c], WF.at[yu, c], sib))
    w_far_up.wait_recv()
    w_sib.append(send(WF.at[y2, c, 0:hr], WF.at[y2, c, 0:hr], sib))
    w_far_down.wait_recv()
    w_sib.append(send(WF.at[y2, c, hr:rows], WF.at[y2, c, hr:rows], sib))

    for copy in cots:
        copy.wait_recv()
    br, bc = iota((512, 512), 0), iota((512, 512), 1)
    back = onehot(bc == (br & 15) * 32 + (br >> 4))
    cot_rows[...] = dot(back, cot_recv[...].reshape(512, 1024)).astype(bf16)

    for copy in w_sib:
        copy.wait_recv()
    for copy in arrive:
        copy.wait_recv()

    px, core, far, near, written = {}, {}, {}, {}, []
    cols = lambda j: slice(starts[j], starts[j] + sizes[j])

    def forward(j):
        part = None
        for kk in range(4):
            a = N[:, :, :, :, kk * chunk:(kk + 1) * chunk].reshape(512, chunk)
            b = WF[kk, :, :, cols(j)].reshape(chunk, sizes[j])
            p = dot(a, b)
            part = p if part is None else part + p
        part = part * scale
        R["acc%d" % j][...] = part
        out, got = R["px_send%d" % j], R["px_recv%d" % j]
        out[...] = part.astype(bf16)
        px[j] = send(out, got, x_pair)

    def pointwise(j):
        px[j].wait_recv()
        pre = R["acc%d" % j][...] + R["px_recv%d" % j][...].astype(f32)
        sig = jax.nn.sigmoid(pre)
        g = cot_rows[:, cols(j)].astype(f32) * sig * (1.0 + pre * (1.0 - sig))
        R["G%d" % j][...] = g.astype(bf16)

    def turned():
        for q in range(half // 256):
            part = N[:, :, :, :, q * 256:(q + 1) * 256].reshape(512, 256)
            NT[q * 256:(q + 1) * 256] = dot(eye, part, 1, 1).astype(bf16)

    order = (2, 1, 3, 0)

    def backward(j):
        g = R["G%d" % j][...]
        CS, CR = R["CS%d" % j], R["CR%d" % j]
        for d in order:
            base = m4(y + d) * chunk
            other = NT[pl.ds(pl.multiple_of(base + (1 - c) * rows, 16), rows)]
            CS[d] = (dot(other, g) * scale).astype(bf16)
            core[j, d] = send(CS.at[d], CR.at[d], sib)
            own = NT[pl.ds(pl.multiple_of(base + c * rows, 16), rows)]
            PB[d, :, :sizes[j]] = dot(own, g) * scale

    def join(j):
        S2, SL, SR, R2, RL, RR = (R["%s%d" % (n, j)] for n in ("S2", "SL", "SR", "R2", "RL", "RR"))
        for d in order:
            core[j, d].wait_recv()
            t = PB[d, :, :sizes[j]] + R["CR%d" % j][d].astype(f32)
            if d == 2:
                S2[...] = t.astype(bf16)
                far[j] = (send(S2.at[0:hr], R2.at[0], up), send(S2.at[hr:rows], R2.at[1], down))
            elif d == 1:
                SL[hr:rows] = t[hr:rows].astype(bf16)
                near[j] = [send(SL.at[hr:rows], RL.at[hr:rows], up)]
                R["keep%d" % j][0] = t[0:hr]
            elif d == 3:
                SR[0:hr] = t[0:hr].astype(bf16)
                near[j].append(send(SR.at[0:hr], RR.at[0:hr], down))
                R["keep%d" % j][1] = t[hr:rows]
            else:
                R["own%d" % j][...] = t

    def pass_on(j):
        SL, SR, R2, RL, RR = (R["%s%d" % (n, j)] for n in ("SL", "SR", "R2", "RL", "RR"))
        far[j][0].wait_recv()
        SL[0:hr] = (R["keep%d" % j][0] + R2[0].astype(f32)).astype(bf16)
        near[j].append(send(SL.at[0:hr], RL.at[0:hr], up))
        far[j][1].wait_recv()
        SR[hr:rows] = (R["keep%d" % j][1] + R2[1].astype(f32)).astype(bf16)
        near[j].append(send(SR.at[hr:rows], RR.at[hr:rows], down))

    def finish(j):
        for copy in near[j]:
            copy.wait_recv()
        grads = R["own%d" % j][...] + R["RL%d" % j][...].astype(f32) + R["RR%d" % j][...].astype(f32)
        stepped = WF[y, c, :, cols(j)].astype(f32) - inner_rate * grads
        for p in range(0, sizes[j], 128):
            f, at = (starts[j] + p) // 256, (starts[j] + p) % 256
            share = due[f][:, :128] * (1.0 - mix_share)
            new = stepped[:, p:p + 128] * (1.0 - share) + share * full_anchor[:, at:at + 128]
            R["out%d" % j][:, p:p + 128] = new.astype(bf16)
        copy = pltpu.make_async_copy(R["out%d" % j], out_hbm.at[:, cols(j)], lsem.at[3 + j])
        copy.start()
        written.append(copy)

    def outer_update():
        for copy in frags:
            copy.wait_recv()
        mean = f_recv[0].astype(f32)
        for i in range(1, 8):
            mean += f_recv[i].astype(f32)
        mean = mean[:, :rows] / 8
        anchor = anchor_ref[...]
        delta = anchor - mean
        new_mom = outer_decay * mom_ref[...] + delta
        new_anchor = anchor - outer_rate * (delta + outer_decay * new_mom)
        new_mom_ref[...] = new_mom
        new_anchor_ref[...] = new_anchor
        a_send[:, rows:] = jnp.zeros((32, a_send.shape[1] - rows), bf16)
        a_send[:, :rows] = new_anchor.astype(bf16)
        anchors = [send(a_send, a_recv.at[w], (worker_of(d, e), s)) for d, e in workers]
        a_recv[w] = a_send[...]
        return anchors

    def outer_spread():
        for copy in anchors:
            copy.wait_recv()
        full_anchor[...] = dot(a_recv[...].reshape(256, 512), eye, 0, 0)[:rows]

    for j in range(n_cols):
        forward(j)
    turned()
    pointwise(0)
    backward(0)
    join(0)
    for j in range(1, n_cols):
        pointwise(j)
        backward(j)
        join(j)
        pass_on(j - 1)
        if j == 1:
            anchors = outer_update()
        if j == 3:
            outer_spread()
        if j >= 3:
            finish(j - 3)
    finish(n_cols - 3)
    pass_on(n_cols - 1)
    finish(n_cols - 2)
    finish(n_cols - 1)
    for copy in written:
        copy.wait()
    done()


def shards(token_ids, cotangent, embedding, weight, anchor, momentum, due_fragment):
    rows, width = weight.shape[1], embedding.shape[1]
    half = width // 2
    vmem = pl.BlockSpec(memory_space=pltpu.VMEM)
    anyspace = pl.BlockSpec(memory_space=pl.ANY)
    V, DMA = pltpu.VMEM, pltpu.SemaphoreType.DMA
    sizes = (128, 128, 256, 256, 128, 128)
    n_sends = 200
    scratch = {
        "emb": V((128, width), bf16),
        "normed": V((128, width), bf16),
        "cot": V((256, 1024), bf16),
        "ids_g": V((8, 8, 256), i32),
        "ids_all": V((16, 8, 256), i32),
        "SS": V((2, 4, 4, 16, half), bf16),
        "RA": V((4, 4, 16, half), bf16),
        "RB": V((4, 4, 16, half), bf16),
        "N": V((4, 4, 2, 16, half), bf16),
        "NT": V((half, 512), bf16),
        "WF": V((4, 2, rows, 1024), bf16),
        "cot_send": V((8, 32, 1024), bf16),
        "cot_far": V((8, 32, 1024), bf16),
        "cot_recv": V((16, 32, 1024), bf16),
        "cot_rows": V((512, 1024), bf16),
        "fpad": V((512, 256), bf16),
        "f_send": V((8, 32, 512), bf16),
        "f_recv": V((8, 32, 512), bf16),
        "a_send": V((32, 512), bf16),
        "a_recv": V((8, 32, 512), bf16),
        "full_anchor": V((rows, 256), f32),
        "PB": V((4, rows, 256), f32),
        "lsem": DMA((3 + len(sizes),)),
        "ssem": DMA((n_sends,)),
        "rsem": DMA((n_sends,)),
    }
    for j, n in enumerate(sizes):
        scratch["acc%d" % j] = V((512, n), f32)
        scratch["px_send%d" % j] = V((512, n), bf16)
        scratch["px_recv%d" % j] = V((512, n), bf16)
        scratch["G%d" % j] = V((512, n), bf16)
        scratch["keep%d" % j] = V((2, rows // 2, n), f32)
        scratch["CS%d" % j] = V((4, rows, n), bf16)
        scratch["CR%d" % j] = V((4, rows, n), bf16)
        scratch["R2%d" % j] = V((2, rows // 2, n), bf16)
        scratch["own%d" % j] = V((rows, n), f32)
        for name in ("S2", "SL", "SR", "RL", "RR", "out"):
            scratch["%s%d" % (name, j)] = V((rows, n), bf16)
    new_weight, new_anchor, new_momentum = pl.pallas_call(
        functools.partial(kernel, tuple(scratch), sizes),
        out_shape=(
            jax.ShapeDtypeStruct((rows, 1024), bf16),
            jax.ShapeDtypeStruct(anchor.shape[::-1], f32),
            jax.ShapeDtypeStruct(anchor.shape[::-1], f32),
        ),
        in_specs=[vmem, pl.BlockSpec(memory_space=pltpu.SMEM), vmem, vmem] + [anyspace] * 3,
        out_specs=(anyspace, vmem, vmem),
        scratch_shapes=list(scratch.values()),
        compiler_params=pltpu.CompilerParams(
            collective_id=0, has_side_effects=True, vmem_limit_bytes=60 * 2**20
        ),
        cost_estimate=pl.CostEstimate(flops=7_500_000_000, bytes_accessed=5_000_000, transcendentals=262144),
        name="diloco_step",
    )(token_ids.reshape(1, 256), due_fragment, anchor.T, momentum.T, embedding, weight.reshape(rows, 1024), cotangent)
    return (new_weight[None], new_anchor.T, new_momentum.T)


def solution(mesh):
    placed = (
        P(("worker", "shard")),
        P(("worker", "shard"), None),
        P(("worker", "shard"), None),
        P("worker", "shard", None),
        P("shard", "worker"),
        P("shard", "worker"),
        P(),
    )
    return jax.shard_map(
        shards,
        mesh=mesh,
        in_specs=placed,
        out_specs=(P("worker", "shard", None), P("shard", "worker"), P("shard", "worker")),
        check_vma=False,
    )
```

time: 139 us -> 122 us (0.88)
  Pallas kernels: 128 us -> 117 us
  local copies, waits for them, and re-layouts: 9.4 us -> 3.46 us
    pallas_call x1, Pallas kernels: 128 us -> 117 us  [shards(): pl.pallas_call(functools.partial(kernel, tuple(scratch), sizes), out_shap...]
    unnamed x5 -> x7, local copies, waits for them, and re-layouts: 8.84 us -> 3.46 us
where the time goes in v2:
time: 122 us
  Pallas kernels  117 us (96%)
  local copies, waits for them, and re-layouts  3.46 us (3%)
  between operations  1.31 us (1%)
    pallas_call x1, Pallas kernels, shards(): pl.pallas_call(functools.partial(kernel, tuple(scratch), sizes), out_shap...  117 us
    unnamed x7, local copies, waits for them, and re-layouts  3.46 us

profile of v2, /device:TPU:1, one launch (start us, length us, event | category | flops | bytes accessed | tf_op | source)
XLA Modules:
  0.0 121.5 jit_solution(9324798227471562943)
XLA Ops:
  1.3 116.8 %diloco_step.1 = (bf16[448,1024]{1,0:T(8,128)(2,1)}, f32[32,448]{1,0:T(8,128)}, f32[32,448]{1,0:T(8,128)}) custom-call(s32[1,256]{1,0:T(1,128)} %bitcast.13, s32[1]{0:T(128)S(6)} %copy.13.due_ref, f32[32,448]{1,0:T(8,128)} %bitcast.11, f32[32,448]{1,0:T(8,128)} %bitcast.12, bf16[128,7168]{1,0:T(8,128)(2,1)} %emb_hbm.1, bf16[448,1024]{1,0:T(8,128)(2,1)} %bitcast.10, ...), custom_call_target="tpu_custom_call" | custom-call | flops 7500000256 | bytes 5000000 | tf_op jit(solution)/shard_map/diloco_step/pallas_call | solution.py:443
  118.0 0.0 copy-start.1
  118.1 0.0 copy-start
  118.1 2.2 %copy.14 = bf16[1,448,1024]{2,1,0:T(8,128)(2,1)} copy(bf16[1,448,1024]{2,1,0:T(8,128)(2,1)} %bitcast.7) | data formatting | bytes 1835008
  120.3 0.0 copy-done.1
  120.3 0.6 copy.15
  120.9 0.0 copy-done
  120.9 0.6 copy.16
Async XLA Ops:
  118.0 2.2 %copy-start.1 = (f32[32,448]{1,0:T(8,128)S(1)}, f32[32,448]{1,0:T(8,128)}, u32[]{:S(2)}) copy-start(f32[32,448]{1,0:T(8,128)} %get-tuple-element.7) | copy-start | bytes 172036
  118.1 2.8 %copy-start = (f32[32,448]{1,0:T(8,128)S(1)}, f32[32,448]{1,0:T(8,128)}, u32[]{:S(2)}) copy-start(f32[32,448]{1,0:T(8,128)} %get-tuple-element.8) | copy-start | bytes 172036

commit v3 on v2

--- a/solution.py
+++ b/solution.py
@@ -131,7 +131,7 @@
     cot_send[...] = dot(onehot(er == place), cot[...]).astype(bf16).reshape(cot_send.shape)
     x_pair = (w, y * 4 + (1 - x_hi) * 2 + c)
     s_pair = s + 2 - 4 * x_hi
-    cot_x = [send(cot_send.at[0:3], cot_far.at[0:3], x_pair)]
+    cot_x = [send(cot_send.at[0:4], cot_far.at[0:4], x_pair)]
     lines = [(d, k) for d in (2, 1, 3, 0) for k in (1, 0) if (d, k) != (0, 0)]
     pair_of = lambda d, k: m4(y + d) * 2 + lax.rem(c + k, 2)
     line_of = lambda d, k: (w, m4(y + d) * 4 + x_hi * 2 + lax.rem(c + k, 2))
@@ -146,8 +146,14 @@
     ids_all[s] = tile
     second = [send(ids_all.at[s], ids_all.at[s], (w, shard_of(*o))) for o in shards]
 
-    cot_x.append(send(cot_send.at[3:8], cot_far.at[3:8], x_pair))
+    cot_x.append(send(cot_send.at[4:8], cot_far.at[4:8], x_pair))
     weight_copy.wait()
+    sib = (w, s + 1 - 2 * c)
+    up, down = (w, m4(y + 1) * 4 + lax.rem(s, 4)), (w, m4(y + 3) * 4 + lax.rem(s, 4))
+    w_up = send(WF.at[y, c], WF.at[y, c], up)
+    w_down = send(WF.at[y, c], WF.at[y, c], down)
+    w_sib = [send(WF.at[y, c], WF.at[y, c], sib)]
+
     fcol = jnp.full((1, 256), lax.rem(due_ref[0], 4), i32)
     due = [jnp.where(fcol == j, 1.0, 0.0) for j in range(4)]
     own_w = WF.at[y, c]
@@ -159,7 +165,6 @@
     eye = onehot(er == ec)
     f_send[...] = dot(eye, fpad[...], 1, 1).astype(bf16).reshape(f_send.shape)
     f_recv[w] = f_send[w]
-    frags = [send(f_send.at[worker_of(d, e)], f_recv.at[w], (worker_of(d, e), s)) for d, e in workers]
 
     emb_copy.wait()
     n_rows = emb.shape[0]
@@ -214,12 +219,6 @@
     N[x, z, 0] = SS[0, z, x]
     N[x, z, 1] = SS[1, x, z]
 
-    sib = (w, s + 1 - 2 * c)
-    up, down = (w, m4(y + 1) * 4 + lax.rem(s, 4)), (w, m4(y + 3) * 4 + lax.rem(s, 4))
-    w_up = send(WF.at[y, c], WF.at[y, c], up)
-    w_down = send(WF.at[y, c], WF.at[y, c], down)
-    w_sib = [send(WF.at[y, c], WF.at[y, c], sib)]
-
     for copy in cot_x:
         copy.wait_recv()
     cots += [send(cot_far.at[pair_of(*o)], cot_recv.at[s_pair], line_of(*o)) for o in lines]
@@ -369,6 +368,7 @@
 
     for j in range(n_cols):
         forward(j)
+    frags = [send(f_send.at[worker_of(d, e)], f_recv.at[w], (worker_of(d, e), s)) for d, e in workers]
     turned()
     pointwise(0)
     backward(0)
@@ -378,16 +378,14 @@
         backward(j)
         join(j)
         pass_on(j - 1)
-        if j == 1:
+        if j == n_cols - 2:
             anchors = outer_update()
-        if j == 3:
-            outer_spread()
-        if j >= 3:
-            finish(j - 3)
-    finish(n_cols - 3)
+    outer_spread()
+    for j in range(n_cols - 3):
+        finish(j)
     pass_on(n_cols - 1)
-    finish(n_cols - 2)
-    finish(n_cols - 1)
+    for j in range(n_cols - 3, n_cols):
+        finish(j)
     for copy in written:
         copy.wait()
     done()

time: 122 us -> 119 us (0.975)
  Pallas kernels: 117 us -> 114 us
    pallas_call x1, Pallas kernels: 117 us -> 114 us  [shards(): pl.pallas_call(functools.partial(kernel, tuple(scratch), sizes), out_shap...]
where the time goes in v3:
time: 119 us
  Pallas kernels  114 us (96%)
  local copies, waits for them, and re-layouts  3.46 us (3%)
  between operations  1.31 us (1%)
    pallas_call x1, Pallas kernels, shards(): pl.pallas_call(functools.partial(kernel, tuple(scratch), sizes), out_shap...  114 us
    unnamed x7, local copies, waits for them, and re-layouts  3.46 us

profile of v3, /device:TPU:1, one launch (start us, length us, event | category | flops | bytes accessed | tf_op | source)
XLA Modules:
  0.0 118.9 jit_solution(9510460713783808508)
XLA Ops:
  1.3 114.1 %diloco_step.1 = (bf16[448,1024]{1,0:T(8,128)(2,1)}, f32[32,448]{1,0:T(8,128)}, f32[32,448]{1,0:T(8,128)}) custom-call(s32[1,256]{1,0:T(1,128)} %bitcast.13, s32[1]{0:T(128)S(6)} %copy.13.due_ref, f32[32,448]{1,0:T(8,128)} %bitcast.11, f32[32,448]{1,0:T(8,128)} %bitcast.12, bf16[128,7168]{1,0:T(8,128)(2,1)} %emb_hbm.1, bf16[448,1024]{1,0:T(8,128)(2,1)} %bitcast.10, ...), custom_call_target="tpu_custom_call" | custom-call | flops 7500000256 | bytes 5000000 | tf_op jit(solution)/shard_map/diloco_step/pallas_call | solution.py:441
  115.4 0.0 copy-start.1
  115.4 0.0 copy-start
  115.4 2.2 %copy.14 = bf16[1,448,1024]{2,1,0:T(8,128)(2,1)} copy(bf16[1,448,1024]{2,1,0:T(8,128)(2,1)} %bitcast.7) | data formatting | bytes 1835008
  117.6 0.0 copy-done.1
  117.6 0.6 copy.15
  118.2 0.0 copy-done
  118.2 0.6 copy.16
Async XLA Ops:
  115.4 2.2 %copy-start.1 = (f32[32,448]{1,0:T(8,128)S(1)}, f32[32,448]{1,0:T(8,128)}, u32[]{:S(2)}) copy-start(f32[32,448]{1,0:T(8,128)} %get-tuple-element.7) | copy-start | bytes 172036
  115.4 2.8 %copy-start = (f32[32,448]{1,0:T(8,128)S(1)}, f32[32,448]{1,0:T(8,128)}, u32[]{:S(2)}) copy-start(f32[32,448]{1,0:T(8,128)} %get-tuple-element.8) | copy-start | bytes 172036

commit v4 on v3

--- a/solution.py
+++ b/solution.py
@@ -35,8 +35,8 @@
 
 def kernel(
     names, sizes,
-    ids_ref, due_ref, anchor_ref, mom_ref, emb_hbm, weight_hbm, cot_hbm,
-    out_hbm, new_anchor_ref, new_mom_ref, *scratch,
+    ids_hbm, due_hbm, anchor_hbm, mom_hbm, emb_hbm, weight_hbm, cot_hbm,
+    out_hbm, new_anchor_hbm, new_mom_hbm, *scratch,
 ):
     R = dict(zip(names, scratch))
     emb, normed, cot, ids_g, ids_all = (R[n] for n in ("emb", "normed", "cot", "ids_g", "ids_all"))
@@ -45,6 +45,8 @@
     fpad, f_send, f_recv = (R[n] for n in ("fpad", "f_send", "f_recv"))
     a_send, a_recv, full_anchor = (R[n] for n in ("a_send", "a_recv", "full_anchor"))
     PB = R["PB"]
+    small = ("ids", "due", "anchor", "mom", "new_anchor", "new_mom")
+    ids_ref, due_ref, anchor_ref, mom_ref, new_anchor_ref, new_mom_ref = (R[n] for n in small)
     lsem, ssem, rsem = R["lsem"], R["ssem"], R["rsem"]
     n_cols = len(sizes)
     starts = [sum(sizes[:j]) for j in range(n_cols)]
@@ -96,6 +98,15 @@
     emb_copy = pltpu.make_async_copy(emb_hbm, emb, lsem.at[0])
     weight_copy = pltpu.make_async_copy(weight_hbm, WF.at[y, c], lsem.at[1])
     cot_copy = pltpu.make_async_copy(cot_hbm, cot, lsem.at[2])
+    at_small = 3 + n_cols
+    small_in = [
+        pltpu.make_async_copy(src, dst, lsem.at[at_small + i])
+        for i, (src, dst) in enumerate(
+            ((ids_hbm, ids_ref), (due_hbm, due_ref), (anchor_hbm, anchor_ref), (mom_hbm, mom_ref))
+        )
+    ]
+    for copy in small_in:
+        copy.start()
     emb_copy.start()
     weight_copy.start()
     cot_copy.start()
@@ -112,6 +123,7 @@
     n_partners += 1
     pl.semaphore_wait(barrier, n_partners)
 
+    small_in[0].wait()
     ids = ids_ref[...]
     ids_g[w] = jnp.broadcast_to(ids, (8, 256))
     first = [send(ids_g.at[w], ids_g.at[w], (worker_of(d, e), s)) for d, e in workers]
@@ -154,6 +166,8 @@
     w_down = send(WF.at[y, c], WF.at[y, c], down)
     w_sib = [send(WF.at[y, c], WF.at[y, c], sib)]
 
+    for copy in small_in[1:]:
+        copy.wait()
     fcol = jnp.full((1, 256), lax.rem(due_ref[0], 4), i32)
     due = [jnp.where(fcol == j, 1.0, 0.0) for j in range(4)]
     own_w = WF.at[y, c]
@@ -355,6 +369,10 @@
         new_anchor = anchor - outer_rate * (delta + outer_decay * new_mom)
         new_mom_ref[...] = new_mom
         new_anchor_ref[...] = new_anchor
+        for i, (src, dst) in enumerate(((new_anchor_ref, new_anchor_hbm), (new_mom_ref, new_mom_hbm))):
+            copy = pltpu.make_async_copy(src, dst, lsem.at[at_small + 4 + i])
+            copy.start()
+            written.append(copy)
         a_send[:, rows:] = jnp.zeros((32, a_send.shape[1] - rows), bf16)
         a_send[:, :rows] = new_anchor.astype(bf16)
         anchors = [send(a_send, a_recv.at[w], (worker_of(d, e), s)) for d, e in workers]
@@ -394,7 +412,6 @@
 def shards(token_ids, cotangent, embedding, weight, anchor, momentum, due_fragment):
     rows, width = weight.shape[1], embedding.shape[1]
     half = width // 2
-    vmem = pl.BlockSpec(memory_space=pltpu.VMEM)
     anyspace = pl.BlockSpec(memory_space=pl.ANY)
     V, DMA = pltpu.VMEM, pltpu.SemaphoreType.DMA
     sizes = (128, 128, 256, 256, 128, 128)
@@ -422,7 +439,13 @@
         "a_recv": V((8, 32, 512), bf16),
         "full_anchor": V((rows, 256), f32),
         "PB": V((4, rows, 256), f32),
-        "lsem": DMA((3 + len(sizes),)),
+        "ids": V((1, 256), i32),
+        "due": pltpu.SMEM((1,), i32),
+        "anchor": V(anchor.shape[::-1], f32),
+        "mom": V(anchor.shape[::-1], f32),
+        "new_anchor": V(anchor.shape[::-1], f32),
+        "new_mom": V(anchor.shape[::-1], f32),
+        "lsem": DMA((9 + len(sizes),)),
         "ssem": DMA((n_sends,)),
         "rsem": DMA((n_sends,)),
     }
@@ -445,8 +468,8 @@
             jax.ShapeDtypeStruct(anchor.shape[::-1], f32),
             jax.ShapeDtypeStruct(anchor.shape[::-1], f32),
         ),
-        in_specs=[vmem, pl.BlockSpec(memory_space=pltpu.SMEM), vmem, vmem] + [anyspace] * 3,
-        out_specs=(anyspace, vmem, vmem),
+        in_specs=[anyspace] * 7,
+        out_specs=(anyspace,) * 3,
         scratch_shapes=list(scratch.values()),
         compiler_params=pltpu.CompilerParams(
             collective_id=0, has_side_effects=True, vmem_limit_bytes=60 * 2**20

time: 119 us -> 118 us (level)
    pallas_call x1, Pallas kernels: 114 us -> 113 us  [shards(): pl.pallas_call(functools.partial(kernel, tuple(scratch), sizes), out_shap...]
where the time goes in v4:
time: 118 us; the launch traced here: 117 us
  Pallas kernels  113 us (96%)
  local copies, waits for them, and re-layouts  3.46 us (3%)
  between operations  1.31 us (1%)
    pallas_call x1, Pallas kernels, shards(): pl.pallas_call(functools.partial(kernel, tuple(scratch), sizes), out_shap...  113 us
    unnamed x7, local copies, waits for them, and re-layouts  3.46 us

profile of v4, /device:TPU:1, one launch (start us, length us, event | category | flops | bytes accessed | tf_op | source)
XLA Modules:
  0.0 117.4 jit_solution(18178235532262845920)
XLA Ops:
  1.3 112.7 %diloco_step.1 = (bf16[448,1024]{1,0:T(8,128)(2,1)}, f32[32,448]{1,0:T(8,128)}, f32[32,448]{1,0:T(8,128)}) custom-call(s32[1,256]{1,0:T(1,128)} %bitcast.13, s32[1]{0:T(128)S(6)} %copy.13.due_hbm, f32[32,448]{1,0:T(8,128)} %bitcast.11, f32[32,448]{1,0:T(8,128)} %bitcast.12, bf16[128,7168]{1,0:T(8,128)(2,1)} %emb_hbm.1, bf16[448,1024]{1,0:T(8,128)(2,1)} %bitcast.10, ...), custom_call_target="tpu_custom_call" | custom-call | flops 7500000256 | bytes 5000000 | tf_op jit(solution)/shard_map/diloco_step/pallas_call | solution.py:464
  113.9 0.0 copy-start.1
  114.0 0.0 copy-start
  114.0 2.2 %copy.14 = bf16[1,448,1024]{2,1,0:T(8,128)(2,1)} copy(bf16[1,448,1024]{2,1,0:T(8,128)(2,1)} %bitcast.7) | data formatting | bytes 1835008
  116.2 0.0 copy-done.1
  116.2 0.6 copy.15
  116.8 0.0 copy-done
  116.8 0.6 copy.16
Async XLA Ops:
  113.9 2.2 %copy-start.1 = (f32[32,448]{1,0:T(8,128)S(1)}, f32[32,448]{1,0:T(8,128)}, u32[]{:S(2)}) copy-start(f32[32,448]{1,0:T(8,128)} %get-tuple-element.7) | copy-start | bytes 172036
  114.0 2.8 %copy-start = (f32[32,448]{1,0:T(8,128)S(1)}, f32[32,448]{1,0:T(8,128)}, u32[]{:S(2)}) copy-start(f32[32,448]{1,0:T(8,128)} %get-tuple-element.8) | copy-start | bytes 172036
